TPU v7x, 256 devices: a whole 4x4x8 slice. The times are simulated.
256 devices in a mesh: view: 16 (over z, core), tok: 16 (over y, x).
Axes of the slice: x: 4, y: 4, z: 8, core: 2. Of those that a mesh axis runs over, the one named last changes fastest.
Arguments:
- queries: bfloat16 [6144, 1024], P('tok'), may hold values from -42 to 42
- keys: bfloat16 [16384, 1024], P('view'), may hold values from -16 to 16
- values: bfloat16 [16384, 1024], P('view'), may hold values from -6 to 6
- grad_out: bfloat16 [6144, 1024], P('tok'), may hold values from -6 to 6
- lengths: int32 [16], P('view'), may hold values from 1 to 1024, 10240 in all
Outputs:
- query_grad: bfloat16 [6144, 1024], P(('tok', 'view'))
- key_grad: bfloat16 [16384, 1024], P(('view', 'tok'))
- value_grad: bfloat16 [16384, 1024], P(('view', 'tok'))
Inputs may be any that keep to these rules, and one draw needn't show every extreme that they name: `lengths`: every view has at least one valid patch; some view has all 1024.
All inputs are finite; a program needn't handle non-finite values. No bound on the sum of `lengths` on one device may be relied on, other than what follows from the above.
Results may differ from a plain program's by a relative error of at most 0.019.
Values may be sent and summed in bfloat16 or wider, within the bound.
A program may use at most 128 MiB of HBM per device.

v0:
```python
import jax
import jax.numpy as jnp
from jax import lax
from jax.sharding import PartitionSpec as P

HEAD = 64


def to_items(matrix, blocks, heads_here):
    rows = matrix.shape[0] // blocks
    shaped = matrix.reshape(blocks, rows, heads_here, HEAD).transpose(2, 0, 1, 3)
    return shaped.reshape(heads_here * blocks, rows, HEAD)


def from_items(items, blocks, heads_here):
    rows = items.shape[1]
    shaped = items.reshape(heads_here, blocks, rows, HEAD).transpose(1, 2, 0, 3)
    return shaped.reshape(blocks * rows, heads_here * HEAD)


def key_items(matrix, blocks, heads_here):
    shaped = matrix.reshape(matrix.shape[0], heads_here, HEAD).transpose(1, 0, 2)
    return jnp.repeat(shaped, blocks, axis=0)


def key_back(items, blocks, heads_here):
    rows = items.shape[1]
    summed = jnp.sum(items.reshape(heads_here, blocks, rows, HEAD), axis=1)
    return summed.transpose(1, 0, 2).reshape(rows, heads_here * HEAD)


def masked_scores(q_item, k_item, valid, scale):
    scores = jnp.einsum("qd,kd->qk", q_item, k_item, preferred_element_type=jnp.float32) * scale
    return jnp.where(valid[None, :], scores, jnp.float32(-1e30))


def local(queries, keys, values, grad_out, lengths):
    scale = HEAD ** (-0.5)
    key_count = keys.shape[0]
    blocks = 1
    q_cols, g_cols, k_cols, v_cols = (queries, grad_out, keys, values)
    heads_here = q_cols.shape[1] // HEAD
    q_items = to_items(q_cols, blocks, heads_here)
    g_items = to_items(g_cols, blocks, heads_here)
    k_items = key_items(k_cols, blocks, heads_here)
    v_items = key_items(v_cols, blocks, heads_here)
    valid = jnp.arange(key_count, dtype=jnp.int32) < lengths[0]

    def local_stats(items):
        q_item, k_item = items
        scores = masked_scores(q_item, k_item, valid, scale)
        top = jnp.max(scores, axis=1)
        return (top, jnp.sum(jnp.exp(scores - top[:, None]), axis=1))

    def local_delta(items):
        q_item, k_item, v_item, g_item, top, total = items
        scores = masked_scores(q_item, k_item, valid, scale)
        probs = jnp.exp(scores - top[:, None]) / total[:, None]
        dprobs = jnp.einsum("qd,kd->qk", g_item, v_item, preferred_element_type=jnp.float32)
        return jnp.sum(probs * dprobs, axis=1)

    top_local, total_local = lax.map(local_stats, (q_items, k_items))
    row_top = lax.pmax(top_local, "view")
    row_sum = lax.psum(total_local * jnp.exp(top_local - row_top), "view")
    delta_local = lax.map(local_delta, (q_items, k_items, v_items, g_items, row_top, row_sum))
    delta = lax.psum(delta_local, "view")

    def local_grads(items):
        q_item, k_item, v_item, g_item, top, total, row_delta = items
        scores = masked_scores(q_item, k_item, valid, scale)
        probs = jnp.exp(scores - top[:, None]) / total[:, None]
        dprobs = jnp.einsum("qd,kd->qk", g_item, v_item, preferred_element_type=jnp.float32)
        dscores = (probs * (dprobs - row_delta[:, None]) * scale).astype(jnp.bfloat16)
        probs_low = probs.astype(jnp.bfloat16)
        grad_q = jnp.einsum("qk,kd->qd", dscores, k_item, preferred_element_type=jnp.float32)
        grad_k = jnp.einsum("qk,qd->kd", dscores, q_item, preferred_element_type=jnp.float32)
        grad_v = jnp.einsum("qk,qd->kd", probs_low, g_item, preferred_element_type=jnp.float32)
        return (grad_q, grad_k, grad_v)

    dq_items, dk_items, dv_items = lax.map(
        local_grads, (q_items, k_items, v_items, g_items, row_top, row_sum, delta)
    )
    dq_cols = from_items(dq_items, blocks, heads_here)
    dk_cols = key_back(dk_items, blocks, heads_here)
    dv_cols = key_back(dv_items, blocks, heads_here)
    key_sum, value_sum = (
        lax.psum_scatter(
            dk_cols.astype(jnp.bfloat16), "tok", scatter_dimension=0, tiled=True
        ).astype(jnp.float32),
        lax.psum_scatter(
            dv_cols.astype(jnp.bfloat16), "tok", scatter_dimension=0, tiled=True
        ).astype(jnp.float32),
    )
    key_grad = key_sum.astype(jnp.bfloat16)
    value_grad = value_sum.astype(jnp.bfloat16)
    query_grad = lax.psum_scatter(dq_cols, "view", scatter_dimension=0, tiled=True).astype(
        jnp.bfloat16
    )
    return (query_grad, key_grad, value_grad)


def solution(mesh):
    in_specs = (P("tok", None), P("view", None), P("view", None), P("tok", None), P("view"))
    out_specs = (P(("tok", "view"), None), P(("view", "tok"), None), P(("view", "tok"), None))
    return jax.shard_map(local, mesh=mesh, in_specs=in_specs, out_specs=out_specs, check_vma=False)
```

profile of v0, /device:TPU:1, one launch (start us, length us, event | category | flops | bytes accessed | tf_op | source)
XLA Modules:
  0.0 638.4 jit_solution(184212100803411453)
XLA Ops:
  12.3 2.9 copy.29
  15.1 3.2 copy.39
  18.3 42.7 %while.39 = (s32[]{:T(128)}, f32[16,384]{1,0:T(8,128)S(1)}, f32[16,384]{1,0:T(8,128)S(1)}, bf16[16,384,64]{2,1,0:T(8,128)(2,1)}, bf16[16,1024,64]{2,1,0:T(8,128)(2,1)}, /*index=5*/s32[]{:T(128)}, s32[]{:T(128)}, s32[]{:T(128)}) while((s32[]{:T(128)}, f32[16,384]{1,0:T(8,128)S(1)}, f32[16,384]{1,0:T(8,128)S(1)}, ...), condition=%wide.region_3.4_spmd.clone, body=%wide.region_0.3_spmd.clone.sunk | while | flops 52297984 | bytes 3526249 | solution.py:62
  61.0 48.8 %pmax.7 = f32[16,384]{1,0:T(8,128)S(1)} all-reduce(f32[16,384]{1,0:T(8,128)S(1)} %get-tuple-element.147), channel_id=1, replica_groups=mesh['view'=16,'tok'=16] {'view'}, use_global_device_ids=true, to_apply=%region_4.5 | all-reduce | flops 6144 | bytes 49152 | tf_op jit(solution)/shard_map/pmax | solution.py:63
  109.8 45.7 %psum.14 = f32[16,384]{1,0:T(8,128)S(1)} all-reduce(f32[16,384]{1,0:T(8,128)S(1)} %exponential_multiply_fusion), channel_id=1, replica_groups=mesh['view'=16,'tok'=16] {'view'}, use_global_device_ids=true, to_apply=%region_5.6 | all-reduce | flops 6144 | bytes 49152 | tf_op jit(solution)/shard_map/psum | solution.py:64
  155.5 2.9 copy.33
  158.4 3.2 copy.41
  161.6 60.6 %while.40 = (s32[]{:T(128)}, f32[16,384]{1,0:T(8,128)S(1)}, bf16[16,384,64]{2,1,0:T(8,128)(2,1)}, bf16[16,1024,64]{2,1,0:T(8,128)(2,1)}, f32[16,384]{1,0:T(8,128...) while((s32[]{:T(128)}, f32[16,384]{1,0:T(8,128)S(1)}, ...), condition=%wide.region_8.9_spmd.clone, body=%wide.region_6.8_spmd.clone.sunk | while | flops 103023232 | bytes 3887745 | solution.py:65
  222.2 45.7 %psum.15 = f32[16,384]{1,0:T(8,128)S(1)} all-reduce(f32[16,384]{1,0:T(8,128)S(1)} %get-tuple-element.149), channel_id=1, replica_groups=mesh['view'=16,'tok'=16] {'view'}, use_global_device_ids=true, to_apply=%region_9.10 | all-reduce | flops 6144 | bytes 49152 | tf_op jit(solution)/shard_map/psum | solution.py:66
  267.9 137.9 %while.41 = (s32[]{:T(128)}, f32[16,384,64]{1,2,0:T(8,128)}, bf16[16,1024,64]{1,2,0:T(8,128)(2,1)}, bf16[16,1024,64]{1,2,0:T(8,128)(2,1)S(1)}, bf16[16,384,64]{2...) while((s32[]{:T(128)}, f32[16,384,64]{1,2,0:T(8,128)}, ...), condition=%wide.region_11.12_spmd.clone, body=%wide.region_10.11_spmd.clone.sunk | while | flops 255198208 | bytes 8901265 | solution.py:80
  272.7 2.0 fusion.90
  281.3 2.0 fusion.90
  298.6 2.0 fusion.90
  341.6 2.0 fusion.90
  350.2 2.0 fusion.90
  358.9 2.0 fusion.90
  376.1 2.0 fusion.90
  393.4 2.0 fusion.90
  405.8 3.1 copy.45
  408.9 2.6 copy.49
  413.1 2.6 copy.47
  415.7 49.4 %reduce-scatter.10.cloned.1.call-done = f32[24,1024]{1,0:T(8,128)} async-done(((f32[384,1024]{1,0:T(8,128)}), f32[24,1024]{1,0:T(8,128)}) %reduce-scatter.10.cloned.1.call-update) | async-done | bytes 98320
  466.9 82.1 %reduce-scatter.14.cloned.1.call-done = bf16[64,1024]{1,0:T(8,128)(2,1)} async-done(((bf16[1024,1024]{1,0:T(8,128)(2,1)}), bf16[64,1024]{1,0:T(8,128)(2,1)}) %reduce-scatter.14.cloned.1.call-update) | async-done | bytes 131088
  549.0 82.8 %reduce-scatter.12.cloned.1.call-done = bf16[64,1024]{1,0:T(8,128)(2,1)} async-done(((bf16[1024,1024]{1,0:T(8,128)(2,1)}), bf16[64,1024]{1,0:T(8,128)(2,1)}) %reduce-scatter.12.cloned.1.call-update) | async-done | bytes 131088
  (353 shorter events, 232.0 us)
Async XLA Ops:
  7.2 458.0 %reduce-scatter.10.cloned.1.call-start = ((), (), s32[]{:S(2)}) async-start(), calls=%async_computation.3 | async-start | bytes 1671168
  8.7 1.6 copy-start.2
  161.6 106.3 %copy-start = (bf16[16,1024,64]{1,2,0:T(8,128)(2,1)S(1)}, bf16[16,1024,64]{1,2,0:T(8,128)(2,1)}, u32[]{:S(2)}) copy-start(bf16[16,1024,64]{1,2,0:T(8,128)(2,1)} %custom-call.2) | copy-start | bytes 6291460
  408.9 140.2 %reduce-scatter.14.cloned.1.call-start = ((), (), s32[]{:S(2)}) async-start(), calls=%async_computation.5 | async-start | bytes 2228224
  411.5 1.6 copy-start.1
  411.5 220.3 %reduce-scatter.12.cloned.1.call-start = ((), (), s32[]{:S(2)}) async-start(), calls=%async_computation.4 | async-start | bytes 2228224
Sparse Core Ops, SparseCore 0:
  409.0 56.1 reduce-scatter.9
  469.7 79.2 reduce-scatter.13
  553.1 78.6 reduce-scatter.11
where the time goes:
time: 643 us; the launch traced here: 638 us
  waiting for transfers between devices  214 us (33%)
  matrix products  198 us (31%)
  blocking collectives  140 us (22%)
  other arithmetic  37.7 us (6%)
  local copies, waits for them, and re-layouts  32.6 us (5%)
  between operations  13.8 us (2%)
    unnamed x6, waiting for transfers between devices  214 us
    dot_general x48, matrix products, masked_scores(): jnp.einsum('qd,kd->qk', q_item, k_item, preferred_element_type=jnp.float32)  69.7 us
    pmax x1, blocking collectives, local(): row_top = lax.pmax(top_local, 'view')  48.8 us
    psum x1, blocking collectives, local(): delta = lax.psum(delta_local, 'view')  45.7 us
    psum x1, blocking collectives, local(): row_sum = lax.psum(total_local * jnp.exp(top_local - row_top), 'view')  45.7 us
    lt x48, other arithmetic, local(): valid = jnp.arange(key_count, dtype=jnp.int32) < lengths[0]  31.4 us
    dot_general x16, matrix products, local_grads(): jnp.einsum('qk,kd->qd', dscores, k_item, preferred_element_type=jnp.float32)  31.2 us
    dot_general x16, matrix products, local_grads(): jnp.einsum('qk,qd->kd', dscores, q_item, preferred_element_type=jnp.float32)  29.5 us
  transfers between devices with their start and end apart: 3, of which 3 were waited for; matrix products, arithmetic and copies ran while one was open for 1% of the time, Pallas kernels for 0%

commit v1 on v0

v1 whole, which is shorter than its diff:
```python
import functools

import jax
import jax.numpy as jnp
from jax import lax
from jax.experimental import pallas as pl
from jax.experimental.pallas import tpu as pltpu
from jax.sharding import PartitionSpec as P

HEAD = 64
PAIR = 128
ROWS = 384
BLOCK = 2 * ROWS
KEYS = 1024
BOTH = 2 * KEYS
NZ = 8
NT = 16
SLOTS = 4
PIECE = ROWS // NZ
SMALL = PIECE // 2
OUT_KEYS = KEYS // NT
STEP1 = 256
STEP2 = 512
MESH = pl.DeviceIdType.MESH
BF = jnp.bfloat16
F32 = jnp.float32
NN = (((1,), (0,)), ((), ()))


def mm(a, b):
    return lax.dot_general(a, b, NN, preferred_element_type=F32)


def kernel(
    len_ref, q_hbm, g_hbm, k_hbm, v_hbm,
    dq_out, dk_out, dv_out,
    q_v, g_v, k_v, v_v, qt, gt, qg_buf, kv_buf, len_buf,
    k0, v0, kt, vt1, s_ref, w_buf, dkv, stats,
    dq_send, dq_recv, dq_red, dkv_send, dkv_recv, dkv_fin, kv_tiles, dq_tiles,
    load_sem, qg_ssem, qg_rsem, kv_ssem, kv_rsem, st_ssem, st_rsem,
    dq_ssem, dq_rsem, x_ssem, x_rsem, fin_ssem, fin_rsem,
):
    v = lax.axis_index("view")
    t = lax.axis_index("tok")
    z = v // 2
    core = v % 2
    y = t // 4
    par = (t + core) % 2
    mate = (2 * z + 1 - core, t)
    scale = HEAD ** -0.5

    pair_cols = pl.ds(pl.multiple_of(PAIR * (t // 2), PAIR), PAIR)
    loads = [
        pltpu.make_async_copy(k_hbm.at[:, pair_cols], k_v, load_sem.at[0]),
        pltpu.make_async_copy(v_hbm.at[:, pair_cols], v_v, load_sem.at[1]),
        pltpu.make_async_copy(q_hbm, q_v, load_sem.at[2]),
        pltpu.make_async_copy(g_hbm, g_v, load_sem.at[3]),
    ]
    for load in loads:
        load.start()

    barrier = pltpu.get_barrier_semaphore()

    def greet_tok(d, _):
        pl.semaphore_signal(barrier, inc=1, device_id=(v, (t + d) % NT), device_id_type=MESH)
        return 0

    def greet_z(d, _):
        pl.semaphore_signal(
            barrier, inc=1, device_id=(2 * ((z + d) % NZ) + core, t), device_id_type=MESH
        )
        return 0

    lax.fori_loop(1, NT, greet_tok, 0)
    lax.fori_loop(1, NZ, greet_z, 0)
    pl.semaphore_signal(barrier, inc=1, device_id=mate, device_id_type=MESH)

    length = len_ref[0]
    lane = lax.broadcasted_iota(jnp.int32, (1, PAIR), 1)
    left = lane < HEAD
    row = lax.broadcasted_iota(jnp.int32, (KEYS, 1), 0)
    loads[0].wait()
    loads[1].wait()
    even = t % 2 == 0
    k_f = k_v[...].astype(F32)
    v_f = v_v[...].astype(F32)
    k_left = jnp.where(even, k_f, pltpu.roll(k_f, HEAD, 1))
    v_right = jnp.where(even, pltpu.roll(v_f, HEAD, 1), v_f)
    kv = jnp.where(left, k_left, v_right)
    kv = jnp.where(row < length, kv, kv[0:1, :])
    kv_buf[core] = kv.astype(BF)
    len_buf[core] = jnp.full((8, PAIR), length, jnp.int32).astype(F32)

    loads[2].wait()
    loads[3].wait()
    pl.semaphore_wait(barrier, NT - 1 + NZ - 1 + 1)

    kv_copy = pltpu.make_async_remote_copy(
        src_ref=kv_buf.at[core], dst_ref=kv_buf.at[core],
        send_sem=kv_ssem.at[0], recv_sem=kv_rsem.at[0],
        device_id=mate, device_id_type=MESH,
    )
    len_copy = pltpu.make_async_remote_copy(
        src_ref=len_buf.at[core], dst_ref=len_buf.at[core],
        send_sem=kv_ssem.at[1], recv_sem=kv_rsem.at[1],
        device_id=mate, device_id_type=MESH,
    )
    kv_copy.start()
    len_copy.start()

    def qg_copy(which, pair):
        src, dst_rows = ((qt, 0), (gt, HEAD))[which]
        dest = 2 * pair + par
        my_y = t // 4
        my_half = (t // 2) % 2
        return pltpu.make_async_remote_copy(
            src_ref=src.at[pl.ds(pl.multiple_of(HEAD * dest, HEAD), HEAD), :],
            dst_ref=qg_buf.at[
                my_y, dst_rows : dst_rows + HEAD, pl.ds(pl.multiple_of(ROWS * my_half, ROWS), ROWS)
            ],
            send_sem=qg_ssem.at[which, pair],
            recv_sem=qg_rsem.at[which, t // 2],
            device_id=(v, dest),
            device_id_type=MESH,
        )

    def pack(j, _):
        pair = 2 * ((y + j // 2) % 4) + j % 2
        dest = 2 * pair + par
        cols = pl.ds(pl.multiple_of(PAIR * pair, PAIR), PAIR)
        qt[cols, :] = q_v[:, cols].T
        gt[cols, :] = g_v[:, cols].T

        @pl.when(dest != t)
        def _():
            qg_copy(0, pair).start()
            qg_copy(1, pair).start()

        @pl.when(dest == t)
        def _():
            here = pl.ds(pl.multiple_of(HEAD * dest, HEAD), HEAD)
            mine = pl.ds(pl.multiple_of(ROWS * ((t // 2) % 2), ROWS), ROWS)
            qg_buf[y, 0:HEAD, mine] = qt[here, :]
            qg_buf[y, HEAD:PAIR, mine] = gt[here, :]

        return 0

    lax.fori_loop(0, NT // 2, pack, 0)

    kv_copy.wait_recv()
    len_copy.wait_recv()
    col = lax.broadcasted_iota(jnp.int32, (1, KEYS), 1).astype(F32)
    sub = lax.broadcasted_iota(jnp.int32, (HEAD, 1), 0)
    for side in range(2):
        here = slice(side * KEYS, (side + 1) * KEYS)
        tile = kv_buf[side]
        f = tile.astype(F32)
        k0[here, :] = jnp.where(left, f, 0.0).astype(BF)
        v0[here, :] = jnp.where(left, 0.0, f).astype(BF)
        flipped = tile.T.astype(F32)
        okay = jnp.where(col < len_buf[side][0:1, 0:1], 1.0, 0.0)
        kt[:, here] = (flipped[0:HEAD] * okay).astype(BF)
        vt1[HEAD:PAIR, here] = (flipped[HEAD:PAIR] * okay).astype(BF)
        vt1[0:HEAD, here] = jnp.where(sub == 0, okay, 0.0).astype(BF)
    dkv[...] = jnp.zeros_like(dkv)

    def stat_copy(i, to):
        return pltpu.make_async_remote_copy(
            src_ref=stats.at[i, z], dst_ref=stats.at[i, z],
            send_sem=st_ssem.at[i, to], recv_sem=st_rsem.at[i, z],
            device_id=(2 * to + core, t), device_id_type=MESH,
        )

    def stat_arrival(i, frm):
        return pltpu.make_async_remote_copy(
            src_ref=stats.at[i, frm], dst_ref=stats.at[i, frm],
            send_sem=st_ssem.at[i, frm], recv_sem=st_rsem.at[i, frm],
            device_id=(2 * frm + core, t), device_id_type=MESH,
        )

    def dq_copy(i, to):
        return pltpu.make_async_remote_copy(
            src_ref=dq_send.at[i, pl.ds(pl.multiple_of(PIECE * to, PIECE), PIECE), :],
            dst_ref=dq_recv.at[i, z],
            send_sem=dq_ssem.at[i, to], recv_sem=dq_rsem.at[i, z],
            device_id=(2 * to + core, t), device_id_type=MESH,
        )

    def dq_arrival(i, frm):
        return pltpu.make_async_remote_copy(
            src_ref=dq_recv.at[i, frm], dst_ref=dq_recv.at[i, frm],
            send_sem=dq_ssem.at[i, frm], recv_sem=dq_rsem.at[i, frm],
            device_id=(2 * frm + core, t), device_id_type=MESH,
        )

    def block_of(i):
        return (y + 3 * i) % 4

    def scores_phase(i):
        sb = block_of(i)
        slot = i % 2
        for half in range(2):
            source = 4 * sb + 2 * half + par

            @pl.when(source != t)
            def _():
                for which in range(2):
                    pltpu.make_async_remote_copy(
                        src_ref=qt.at[0:HEAD, :],
                        dst_ref=qg_buf.at[
                            sb, which * HEAD : (which + 1) * HEAD, half * ROWS : (half + 1) * ROWS
                        ],
                        send_sem=qg_ssem.at[which, 2 * sb + half],
                        recv_sem=qg_rsem.at[which, 2 * sb + half],
                        device_id=(v, source),
                        device_id_type=MESH,
                    ).wait_recv()

        qg = qg_buf[sb]
        top = jnp.full((8, BLOCK), -3e38, F32)
        for k in range(BOTH // STEP1):
            here = slice(k * STEP1, (k + 1) * STEP1)
            s = mm(k0[here, :], qg)
            s_ref[here, :] = s
            top = jnp.maximum(top, jnp.max(s.reshape(STEP1 // 8, 8, BLOCK), axis=0))
        top = jnp.max(top, axis=0, keepdims=True)
        acc = jnp.zeros((PAIR, BLOCK), F32)
        for k in range(BOTH // STEP1):
            here = slice(k * STEP1, (k + 1) * STEP1)
            w = jnp.exp((s_ref[here, :] - top) * scale).astype(BF)
            w_buf[slot, here, :] = w
            acc = acc + mm(vt1[:, here], w)
        total = acc[0:1, :]
        mean = jnp.sum(acc[HEAD:, :] * qg[HEAD:, :].astype(F32), axis=0, keepdims=True)
        top = top * scale
        mine = stats.at[i, z]
        mine[0:1, :] = top[:, :ROWS]
        mine[1:2, :] = top[:, ROWS:]
        mine[2:3, :] = total[:, :ROWS]
        mine[3:4, :] = total[:, ROWS:]
        mine[4:5, :] = mean[:, :ROWS]
        mine[5:6, :] = mean[:, ROWS:]
        mine[6:8, :] = jnp.zeros((2, ROWS), F32)

        def send(d, _):
            stat_copy(i, (z + d) % NZ).start()
            return 0

        lax.fori_loop(1, NZ, send, 0)

    def grads_phase(i):
        sb = block_of(i)
        slot = i % 2

        def arrive(d, _):
            stat_arrival(i, (z + d) % NZ).wait_recv()
            return 0

        lax.fori_loop(1, NZ, arrive, 0)
        every = stats[i]
        tops = every[:, 0:2, :]
        top = jnp.max(tops, axis=0)
        weight = jnp.exp(tops - top[None])
        total = jnp.sum(every[:, 2:4, :] * weight, axis=0)
        mean = jnp.sum(every[:, 4:6, :] * weight, axis=0) / total
        factor = jnp.exp(stats[i, z, 0:2, :] - top) / total
        mean = jnp.concatenate([mean[0:1], mean[1:2]], axis=1)
        factor = jnp.concatenate([factor[0:1], factor[1:2]], axis=1)

        qg = qg_buf[sb]
        scaled = (qg.astype(F32) * factor).T
        cq = jnp.where(left, scaled * scale, 0.0).astype(BF)
        cg = jnp.where(left, 0.0, scaled).astype(BF)
        acc = jnp.zeros((HEAD, BLOCK), F32)
        for k in range(BOTH // STEP2):
            here = slice(k * STEP2, (k + 1) * STEP2)
            dp = mm(v0[here, :], qg)
            w = w_buf[slot, here, :]
            ds = (w.astype(F32) * (dp - mean)).astype(BF)
            acc = acc + mm(kt[:, here], ds)
            dkv[here, :] += mm(ds, cq) + mm(w, cg)
        acc = acc * (factor * scale)
        two = jnp.concatenate([acc[:, :ROWS], acc[:, ROWS:]], axis=0)
        dq_send[i] = two.T.astype(BF)

        def send(d, _):
            dq_copy(i, (z + d) % NZ).start()
            return 0

        lax.fori_loop(1, NZ, send, 0)

    def turn(i, _):
        @pl.when(i < SLOTS)
        def _():
            scores_phase(i)

        @pl.when(i > 0)
        def _():
            grads_phase(i - 1)

        return 0

    lax.fori_loop(0, SLOTS + 1, turn, 0)

    mate_rows = pl.ds(pl.multiple_of(KEYS * (1 - core), KEYS), KEYS)
    own_rows = pl.ds(pl.multiple_of(KEYS * core, KEYS), KEYS)
    dkv_send[...] = dkv[mate_rows, :].astype(BF)
    dkv_copy = pltpu.make_async_remote_copy(
        src_ref=dkv_send, dst_ref=dkv_recv,
        send_sem=x_ssem.at[0], recv_sem=x_rsem.at[0],
        device_id=mate, device_id_type=MESH,
    )
    dkv_copy.start()

    def reduce(i, _):
        def arrive(d, _):
            dq_arrival(i, (z + d) % NZ).wait_recv()
            return 0

        lax.fori_loop(1, NZ, arrive, 0)
        piece = dq_send[i, pl.ds(pl.multiple_of(PIECE * z, PIECE), PIECE), :].astype(F32)

        def add(d, piece):
            return piece + dq_recv[i, (z + d) % NZ].astype(F32)

        piece = lax.fori_loop(1, NZ, add, piece)
        for c in range(2):
            dq_red[c, par, block_of(i)] = piece[c * SMALL : (c + 1) * SMALL, :]
        return 0

    lax.fori_loop(0, SLOTS, reduce, 0)
    dq_mate = pltpu.make_async_remote_copy(
        src_ref=dq_red.at[1 - core, par], dst_ref=dq_red.at[1 - core, par],
        send_sem=x_ssem.at[1], recv_sem=x_rsem.at[1],
        device_id=mate, device_id_type=MESH,
    )
    dq_mate.start()
    dq_mate_arrival = pltpu.make_async_remote_copy(
        src_ref=dq_red.at[core, 1 - par], dst_ref=dq_red.at[core, 1 - par],
        send_sem=x_ssem.at[1], recv_sem=x_rsem.at[1],
        device_id=mate, device_id_type=MESH,
    )

    dkv_copy.wait_recv()
    whole = dkv[own_rows, :] + dkv_recv[...].astype(F32)
    dkv_fin[...] = jnp.where(row < length, whole, 0.0).astype(BF)

    def kv_out(to, frm):
        return pltpu.make_async_remote_copy(
            src_ref=dkv_fin.at[pl.ds(pl.multiple_of(OUT_KEYS * to, OUT_KEYS), OUT_KEYS), :],
            dst_ref=kv_tiles.at[frm],
            send_sem=fin_ssem.at[0, to], recv_sem=fin_rsem.at[0, frm],
            device_id=(v, to), device_id_type=MESH,
        )

    def dq_out_copy(to, frm):
        return pltpu.make_async_remote_copy(
            src_ref=dq_red.at[core, to % 2, to // 4],
            dst_ref=dq_tiles.at[frm],
            send_sem=fin_ssem.at[1, to], recv_sem=fin_rsem.at[1, frm],
            device_id=(v, to), device_id_type=MESH,
        )

    def send_kv(d, _):
        kv_out((t + d) % NT, t).start()
        return 0

    def send_dq(d, _):
        dq_out_copy((t + d) % NT, t).start()
        return 0

    lax.fori_loop(1, NT, send_kv, 0)
    kv_tiles[t] = dkv_fin[pl.ds(pl.multiple_of(OUT_KEYS * t, OUT_KEYS), OUT_KEYS), :]
    dq_mate_arrival.wait_recv()
    lax.fori_loop(1, NT, send_dq, 0)
    dq_tiles[t] = dq_red[core, t % 2, t // 4]

    def wait_kv(d, _):
        kv_out((t + d) % NT, (t + d) % NT).wait_recv()
        return 0

    def wait_dq(d, _):
        dq_out_copy((t + d) % NT, (t + d) % NT).wait_recv()
        return 0

    lax.fori_loop(1, NT, wait_kv, 0)
    for p in range(NT // 2):
        cols = slice(p * PAIR, (p + 1) * PAIR)
        a = kv_tiles[2 * p].astype(F32)
        b = kv_tiles[2 * p + 1].astype(F32)
        dk_out[:, cols] = jnp.where(left, a, pltpu.roll(b, HEAD, 1)).astype(BF)
        dv_out[:, cols] = jnp.where(left, pltpu.roll(a, HEAD, 1), b).astype(BF)
    lax.fori_loop(1, NT, wait_dq, 0)
    first = (t // 2) % 2 == 0
    for p in range(NT // 2):
        cols = slice(p * PAIR, (p + 1) * PAIR)
        a = dq_tiles[2 * p]
        b = dq_tiles[2 * p + 1]
        a = jnp.where(first, a, pltpu.roll(a, HEAD, 1))
        b = jnp.where(first, pltpu.roll(b, HEAD, 1), b)
        dq_out[:, cols] = jnp.where(left, a, b).astype(BF)

    kv_copy.wait_send()
    len_copy.wait_send()
    dkv_copy.wait_send()
    dq_mate.wait_send()

    def drain_qg(pair, _):
        @pl.when(2 * pair + par != t)
        def _():
            qg_copy(0, pair).wait_send()
            qg_copy(1, pair).wait_send()

        return 0

    def drain_z(d, _):
        to = (z + d) % NZ
        for i in range(SLOTS):
            stat_copy(i, to).wait_send()
            dq_copy(i, to).wait_send()
        return 0

    def drain_fin(d, _):
        to = (t + d) % NT
        kv_out(to, t).wait_send()
        dq_out_copy(to, t).wait_send()
        return 0

    lax.fori_loop(0, NT // 2, drain_qg, 0)
    lax.fori_loop(1, NZ, drain_z, 0)
    lax.fori_loop(1, NT, drain_fin, 0)


def local(queries, keys, values, grad_out, lengths):
    dma = pltpu.SemaphoreType.DMA
    vm = pltpu.VMEM
    return pl.pallas_call(
        kernel,
        out_shape=(
            jax.ShapeDtypeStruct((SMALL, NT * HEAD), BF),
            jax.ShapeDtypeStruct((OUT_KEYS, NT * HEAD), BF),
            jax.ShapeDtypeStruct((OUT_KEYS, NT * HEAD), BF),
        ),
        in_specs=[pl.BlockSpec(memory_space=pltpu.SMEM)]
        + [pl.BlockSpec(memory_space=pl.ANY)] * 4,
        out_specs=(pl.BlockSpec(memory_space=pltpu.VMEM),) * 3,
        scratch_shapes=[
            vm((ROWS, NT * HEAD), BF), vm((ROWS, NT * HEAD), BF),
            vm((KEYS, PAIR), BF), vm((KEYS, PAIR), BF),
            vm((NT * HEAD, ROWS), BF), vm((NT * HEAD, ROWS), BF),
            vm((SLOTS, PAIR, BLOCK), BF),
            vm((2, KEYS, PAIR), BF), vm((2, 8, PAIR), F32),
            vm((BOTH, PAIR), BF), vm((BOTH, PAIR), BF),
            vm((HEAD, BOTH), BF), vm((PAIR, BOTH), BF),
            vm((BOTH, BLOCK), F32), vm((2, BOTH, BLOCK), BF),
            vm((BOTH, PAIR), F32), vm((SLOTS, NZ, 8, ROWS), F32),
            vm((SLOTS, ROWS, PAIR), BF), vm((SLOTS, NZ, PIECE, PAIR), BF),
            vm((2, 2, SLOTS, SMALL, PAIR), F32),
            vm((KEYS, PAIR), BF), vm((KEYS, PAIR), BF), vm((KEYS, PAIR), BF),
            vm((NT, OUT_KEYS, PAIR), BF), vm((NT, SMALL, PAIR), F32),
            dma((4,)), dma((2, NT // 2)), dma((2, NT // 2)), dma((2,)), dma((2,)),
            dma((SLOTS, NZ)), dma((SLOTS, NZ)), dma((SLOTS, NZ)), dma((SLOTS, NZ)),
            dma((2,)), dma((2,)), dma((2, NT)), dma((2, NT)),
        ],
        compiler_params=pltpu.CompilerParams(
            collective_id=0, has_side_effects=True, vmem_limit_bytes=56 * 2**20
        ),
    )(lengths, queries, grad_out, keys, values)


def solution(mesh):
    in_specs = (P("tok", None), P("view", None), P("view", None), P("tok", None), P("view"))
    out_specs = (P(("tok", "view"), None), P(("view", "tok"), None), P(("view", "tok"), None))
    return jax.shard_map(local, mesh=mesh, in_specs=in_specs, out_specs=out_specs, check_vma=False)
```

time: 643 us -> 69.7 us (0.11)
  waiting for transfers between devices: 214 us -> 0 us
  matrix products: 198 us -> 0 us
  blocking collectives: 140 us -> 0 us
  Pallas kernels: 0 us -> 63.6 us
  other arithmetic: 37.7 us -> 0 us
  local copies, waits for them, and re-layouts: 32.6 us -> 4.56 us
  between operations: 13.8 us -> 1.29 us
    unnamed x6 -> x0, waiting for transfers between devices: 214 us -> none
    dot_general x128 -> x0, matrix products: 198 us -> none  [the longest x48 69.7 us: masked_scores(): jnp.einsum('qd,kd->qk', q_item, k_item, preferred_element_type=jnp.float32)]
    psum x2 -> x0, blocking collectives: 91.4 us -> none  [the longest x1 45.7 us: local(): delta = lax.psum(delta_local, 'view')]
    pallas_call x0 -> x1, Pallas kernels: none -> 63.6 us  [local(): pl.pallas_call(kernel, out_shape=(jax.ShapeDtypeStruct((SMALL, NT * HEAD)...]
    pmax x1 -> x0, blocking collectives: 48.8 us -> none  [local(): row_top = lax.pmax(top_local, 'view')]
    lt x48 -> x0, other arithmetic: 31.4 us -> none  [local(): valid = jnp.arange(key_count, dtype=jnp.int32) < lengths[0]]
    unnamed x19 -> x3, local copies, waits for them, and re-layouts: 28.6 us -> 4.56 us
  transfers between devices with their start and end apart: 3 -> 0, of which waited for: 3 -> 0; matrix products, arithmetic and copies ran while one was open for 1% -> 0% of each run, Pallas kernels for 0% -> 0%
where the time goes in v1:
time: 69.7 us; the launch traced here: 69.5 us
  Pallas kernels  63.6 us (91%)
  local copies, waits for them, and re-layouts  4.56 us (7%)
  between operations  1.29 us (2%)
    pallas_call x1, Pallas kernels, local(): pl.pallas_call(kernel, out_shape=(jax.ShapeDtypeStruct((SMALL, NT * HEAD)...  63.6 us
    unnamed x3, local copies, waits for them, and re-layouts  4.56 us

profile of v1, /device:TPU:1, one launch (start us, length us, event | category | flops | bytes accessed | tf_op | source)
XLA Modules:
  0.0 69.5 jit_solution(12823711150862660943)
XLA Ops:
  1.3 63.6 %shard_map.76 = (bf16[24,1024]{1,0:T(8,128)(2,1)}, bf16[64,1024]{1,0:T(8,128)(2,1)}, bf16[64,1024]{1,0:T(8,128)(2,1)}) custom-call(s32[1]{0:T(128)S(6)} %copy.11.len_ref, bf16[384,1024]{1,0:T(8,128)(2,1)} %q_hbm.1, bf16[384,1024]{1,0:T(8,128)(2,1)} %g_hbm.1, bf16[1024,1024]{1,0:T(8,128)(2,1)} %k_hbm.1, bf16[1024,1024]{1,0:T(8,128)(2,1)} %v_hbm.1), custom_call_target="tpu_custom_call" | custom-call | tf_op jit(solution)/shard_map/pallas_call | solution.py:437
  64.9 1.4 %copy.12 = bf16[24,1024]{1,0:T(8,128)(2,1)} copy(bf16[24,1024]{1,0:T(8,128)(2,1)} %get-tuple-element.6) | data formatting | bytes 98304
  66.3 1.6 %copy.13 = bf16[64,1024]{1,0:T(8,128)(2,1)} copy(bf16[64,1024]{1,0:T(8,128)(2,1)} %get-tuple-element.7) | data formatting | bytes 262144
  67.9 1.6 %copy.14 = bf16[64,1024]{1,0:T(8,128)(2,1)} copy(bf16[64,1024]{1,0:T(8,128)(2,1)} %get-tuple-element.8) | data formatting | bytes 262144

commit v2 on v1

v2 whole, which is shorter than its diff:
```python
import functools

import jax
import jax.numpy as jnp
from jax import lax
from jax.experimental import pallas as pl
from jax.experimental.pallas import tpu as pltpu
from jax.sharding import PartitionSpec as P

HEAD = 64
PAIR = 128
ROWS = 384
BLOCK = 2 * ROWS
KEYS = 1024
BOTH = 2 * KEYS
NZ = 8
NT = 16
SLOTS = 4
PIECE = ROWS // NZ
SMALL = PIECE // 2
OUT_KEYS = KEYS // NT
STEP1 = 256
STEP2 = 512
HALF = 512
PAD = 32
MESH = pl.DeviceIdType.MESH
BF = jnp.bfloat16
F32 = jnp.float32
NN = (((1,), (0,)), ((), ()))


def mm(a, b):
    return lax.dot_general(a, b, NN, preferred_element_type=F32)


def kernel(
    len_ref, q_hbm, g_hbm, k_hbm, v_hbm,
    kv_tiles, dq_tiles,
    q_v, g_v, k_v, v_v, turned, qgt, qg_buf, kv_buf, len_buf,
    k0, v0, kt, vt1, s_ref, w_buf, ds_buf, dkv, stats, tops,
    dq_send, dq_recv, dq_fin, dkv_send, dkv_recv, dkv_fin,
    load_sem, qg_ssem, qg_rsem, kv_ssem, kv_rsem, st_ssem, st_rsem,
    dq_ssem, dq_rsem, x_ssem, x_rsem, kvf_ssem, kvf_rsem, dqf_ssem, dqf_rsem, self_sem,
):
    v = lax.axis_index("view")
    t = lax.axis_index("tok")
    z = v // 2
    core = v % 2
    y = t // 4
    par = (t + core) % 2
    other = 2 * z + 1 - core
    scale = HEAD ** -0.5

    pair_cols = pl.ds(pl.multiple_of(PAIR * (t // 2), PAIR), PAIR)
    loads = [
        pltpu.make_async_copy(k_hbm.at[:, pair_cols], k_v, load_sem.at[0]),
        pltpu.make_async_copy(v_hbm.at[:, pair_cols], v_v, load_sem.at[1]),
        pltpu.make_async_copy(q_hbm, q_v, load_sem.at[2]),
        pltpu.make_async_copy(g_hbm, g_v, load_sem.at[3]),
    ]
    for load in loads:
        load.start()

    barrier = pltpu.get_barrier_semaphore()

    def greet(view, tok):
        pl.semaphore_signal(barrier, inc=1, device_id=(view, tok), device_id_type=MESH)

    def greet_tok(d, _):
        greet(v, (t + d) % NT)
        return 0

    def greet_z(d, _):
        greet(2 * ((z + d) % NZ) + core, t)
        return 0

    def greet_other(d, _):
        tok = 2 * d + 1 - par

        @pl.when(tok != t)
        def _():
            greet(other, tok)

        return 0

    greet(other, t)
    lax.fori_loop(1, NT, greet_tok, 0)
    lax.fori_loop(0, NT // 2, greet_other, 0)
    lax.fori_loop(1, NZ, greet_z, 0)

    length = len_ref[0]
    lane = lax.broadcasted_iota(jnp.int32, (1, PAIR), 1)
    left = lane < HEAD
    row = lax.broadcasted_iota(jnp.int32, (KEYS, 1), 0)
    loads[0].wait()
    loads[1].wait()
    even = t % 2 == 0
    k_f = k_v[...].astype(F32)
    v_f = v_v[...].astype(F32)
    k_left = jnp.where(even, k_f, pltpu.roll(k_f, HEAD, 1))
    v_right = jnp.where(even, pltpu.roll(v_f, HEAD, 1), v_f)
    kv = jnp.where(left, k_left, v_right)
    kv = jnp.where(row < length, kv, kv[0:1, :])
    kv_buf[core] = kv.astype(BF)
    len_buf[core] = jnp.full((8, PAIR), length, jnp.int32).astype(F32)

    loads[2].wait()
    loads[3].wait()
    chosen = pl.ds(pl.multiple_of(HEAD * par, HEAD), HEAD)

    def pack(pair, _):
        cols = pl.ds(pl.multiple_of(PAIR * pair, PAIR), PAIR)
        turned[0] = q_v[:, cols].T
        turned[1] = g_v[:, cols].T
        qgt[pair, 0:HEAD, :] = turned[0, chosen, :]
        qgt[pair, HEAD:PAIR, :] = turned[1, chosen, :]
        return 0

    lax.fori_loop(0, NT // 2, pack, 0)

    col = lax.broadcasted_iota(jnp.int32, (1, KEYS), 1).astype(F32)
    sub = lax.broadcasted_iota(jnp.int32, (HEAD, 1), 0)

    def prepare(side):
        here = pl.ds(pl.multiple_of(KEYS * side, KEYS), KEYS)
        tile = kv_buf[side]
        f = tile.astype(F32)
        k0[here, :] = jnp.where(left, f, 0.0).astype(BF)
        v0[here, :] = jnp.where(left, 0.0, f).astype(BF)
        flipped = tile.T.astype(F32)
        okay = jnp.where(col < len_buf[side][0:1, 0:1], 1.0, 0.0)
        kt[:, here] = (flipped[0:HEAD] * okay).astype(BF)
        vt1[HEAD:PAIR, here] = (flipped[HEAD:PAIR] * okay).astype(BF)
        vt1[0:HEAD, here] = jnp.where(sub == 0, okay, 0.0).astype(BF)

    prepare(core)
    dkv[...] = jnp.zeros_like(dkv)

    pl.semaphore_wait(barrier, 1 + NT - 1 + NT // 2 - (1 - core) + NZ - 1)

    kv_copy = pltpu.make_async_remote_copy(
        src_ref=kv_buf.at[core], dst_ref=kv_buf.at[core],
        send_sem=kv_ssem.at[0], recv_sem=kv_rsem.at[0],
        device_id=(other, t), device_id_type=MESH,
    )
    len_copy = pltpu.make_async_remote_copy(
        src_ref=len_buf.at[core], dst_ref=len_buf.at[core],
        send_sem=kv_ssem.at[1], recv_sem=kv_rsem.at[1],
        device_id=(other, t), device_id_type=MESH,
    )
    kv_copy.start()
    len_copy.start()

    def qg_copy(pair):
        return pltpu.make_async_remote_copy(
            src_ref=qgt.at[pair], dst_ref=qg_buf.at[y, (t // 2) % 2],
            send_sem=qg_ssem.at[pair], recv_sem=qg_rsem.at[t // 2],
            device_id=(v, 2 * pair + par), device_id_type=MESH,
        )

    def send_row(j):
        for half in range(2):
            pair = 2 * ((y + j) % 4) + half

            @pl.when(2 * pair + par != t)
            def _():
                qg_copy(pair).start()

            @pl.when(2 * pair + par == t)
            def _():
                qg_buf[y, half] = qgt[pair]

    send_row(0)
    send_row(1)

    kv_copy.wait_recv()
    len_copy.wait_recv()
    prepare(1 - core)

    def stat_copy(i, to, frm):
        return pltpu.make_async_remote_copy(
            src_ref=stats.at[i, frm], dst_ref=stats.at[i, frm],
            send_sem=st_ssem.at[i, to], recv_sem=st_rsem.at[i, frm],
            device_id=(2 * to + core, t), device_id_type=MESH,
        )

    def dq_copy(i, to, frm):
        return pltpu.make_async_remote_copy(
            src_ref=dq_send.at[i, pl.ds(pl.multiple_of(PIECE * to, PIECE), PIECE), :],
            dst_ref=dq_recv.at[i, frm],
            send_sem=dq_ssem.at[i, to], recv_sem=dq_rsem.at[i, frm],
            device_id=(2 * to + core, t), device_id_type=MESH,
        )

    def block_of(i):
        return (y + 3 * i) % 4

    def queries_of(i):
        sb = block_of(i)
        return jnp.concatenate([qg_buf[sb, 0], qg_buf[sb, 1]], axis=1)

    def scores_phase(i):
        sb = block_of(i)
        slot = i % 2
        for half in range(2):
            source = 4 * sb + 2 * half + par

            @pl.when(source != t)
            def _():
                pltpu.make_async_remote_copy(
                    src_ref=qgt.at[0], dst_ref=qg_buf.at[sb, half],
                    send_sem=qg_ssem.at[0], recv_sem=qg_rsem.at[2 * sb + half],
                    device_id=(v, source), device_id_type=MESH,
                ).wait_recv()

        @pl.when(i < 2)
        def _():
            send_row(i + 2)

        qg = queries_of(i)
        top = jnp.full((8, BLOCK), -3e38, F32)
        for k in range(BOTH // STEP1):
            here = slice(k * STEP1, (k + 1) * STEP1)
            s = mm(k0[here, :], qg)
            s_ref[here, :] = s
            top = jnp.maximum(top, jnp.max(s.reshape(STEP1 // 8, 8, BLOCK), axis=0))
        top = jnp.max(top, axis=0, keepdims=True)
        acc = jnp.zeros((PAIR, BLOCK), F32)
        for k in range(BOTH // STEP1):
            here = slice(k * STEP1, (k + 1) * STEP1)
            w = jnp.exp((s_ref[here, :] - top) * scale).astype(BF)
            w_buf[slot, here, :] = w
            acc = acc + mm(vt1[:, here], w)
        total = acc[0:1, :]
        mean = jnp.sum(acc[HEAD:, :] * qg[HEAD:, :].astype(F32), axis=0, keepdims=True)
        top = top * scale
        tops[slot] = top
        stats[i, z, 0:1, :] = top + jnp.log(total)
        stats[i, z, 1:2, :] = mean / total

        def send(d, _):
            stat_copy(i, (z + d) % NZ, z).start()
            return 0

        lax.fori_loop(1, NZ, send, 0)

    def combine(i):
        def arrive(d, _):
            frm = (z + d) % NZ
            stat_copy(i, frm, frm).wait_recv()
            return 0

        lax.fori_loop(1, NZ, arrive, 0)
        logs = stats[i, :, 0, :]
        peak = jnp.max(logs, axis=0, keepdims=True)
        weight = jnp.exp(logs - peak)
        total = jnp.sum(weight, axis=0, keepdims=True)
        mean = jnp.sum(stats[i, :, 1, :] * weight, axis=0, keepdims=True) / total
        factor = jnp.exp(tops[i % 2] - peak) / total
        qg = queries_of(i)
        scaled = (qg.astype(F32) * factor).T
        cq = jnp.where(left, scaled * scale, 0.0).astype(BF)
        cg = jnp.where(left, 0.0, scaled).astype(BF)
        return qg, mean, factor, cq, cg

    def give_dq(i, acc, factor):
        acc = acc * (factor * scale)
        two = jnp.concatenate([acc[:, :ROWS], acc[:, ROWS:]], axis=0)
        dq_send[i] = two.T.astype(BF)

        def send(d, _):
            dq_copy(i, (z + d) % NZ, z).start()
            return 0

        lax.fori_loop(1, NZ, send, 0)

    def grads_phase(i):
        slot = i % 2
        qg, mean, factor, cq, cg = combine(i)
        acc = jnp.zeros((HEAD, BLOCK), F32)
        for k in range(BOTH // STEP2):
            here = slice(k * STEP2, (k + 1) * STEP2)
            dp = mm(v0[here, :], qg)
            w = w_buf[slot, here, :]
            ds = (w.astype(F32) * (dp - mean)).astype(BF)
            acc = acc + mm(kt[:, here], ds)
            dkv[here, :] += mm(ds, cq) + mm(w, cg)
        give_dq(i, acc, factor)

    def dq_give(i, half, c):
        return pltpu.make_async_remote_copy(
            src_ref=dq_fin.at[i, c], dst_ref=dq_tiles.at[t],
            send_sem=dqf_ssem.at[i, half, c], recv_sem=dqf_rsem.at[t],
            device_id=(2 * z + c, 4 * block_of(i) + 2 * half + par), device_id_type=MESH,
        )

    def own_piece(i, half, c):
        return jnp.logical_and(4 * block_of(i) + 2 * half + par == t, c == core)

    def reduce(i):
        def arrive(d, _):
            frm = (z + d) % NZ
            dq_copy(i, frm, frm).wait_recv()
            return 0

        lax.fori_loop(1, NZ, arrive, 0)
        piece = dq_send[i, pl.ds(pl.multiple_of(PIECE * z, PIECE), PIECE), :].astype(F32)

        def add(d, piece):
            return piece + dq_recv[i, (z + d) % NZ].astype(F32)

        piece = lax.fori_loop(1, NZ, add, piece)
        fill = jnp.zeros((PAD - SMALL, PAIR), F32)
        for c in range(2):
            rows = piece[c * SMALL : (c + 1) * SMALL, :]
            dq_fin[i, c] = jnp.concatenate([rows, fill], axis=0).astype(BF)
        for half in range(2):
            for c in range(2):
                @pl.when(jnp.logical_not(own_piece(i, half, c)))
                def _():
                    dq_give(i, half, c).start()

                @pl.when(own_piece(i, half, c))
                def _():
                    keep = pltpu.make_async_copy(dq_fin.at[i, c], dq_tiles.at[t], self_sem.at[0])
                    keep.start()
                    keep.wait()

    def turn(i, _):
        scores_phase(i)

        @pl.when(i > 0)
        def _():
            grads_phase(i - 1)

        @pl.when(i > 1)
        def _():
            reduce(i - 2)

        return 0

    lax.fori_loop(0, SLOTS, turn, 0)

    last = SLOTS - 1
    qg, mean, factor, cq, cg = combine(last)
    acc = jnp.zeros((HEAD, BLOCK), F32)
    for k in range(BOTH // STEP2):
        here = slice(k * STEP2, (k + 1) * STEP2)
        dp = mm(v0[here, :], qg)
        ds = (w_buf[last % 2, here, :].astype(F32) * (dp - mean)).astype(BF)
        ds_buf[here, :] = ds
        acc = acc + mm(kt[:, here], ds)
    give_dq(last, acc, factor)

    def dkv_copy(j):
        return pltpu.make_async_remote_copy(
            src_ref=dkv_send.at[j], dst_ref=dkv_recv.at[j],
            send_sem=x_ssem.at[j], recv_sem=x_rsem.at[j],
            device_id=(other, t), device_id_type=MESH,
        )

    def kv_out(to, frm):
        return pltpu.make_async_remote_copy(
            src_ref=dkv_fin.at[pl.ds(pl.multiple_of(OUT_KEYS * to, OUT_KEYS), OUT_KEYS), :],
            dst_ref=kv_tiles.at[frm],
            send_sem=kvf_ssem.at[to], recv_sem=kvf_rsem.at[frm],
            device_id=(v, to), device_id_type=MESH,
        )

    def kv_total(side, j):
        here = pl.ds(pl.multiple_of(KEYS * side + HALF * j, HALF), HALF)
        return dkv[here, :] + mm(ds_buf[here, :], cq) + mm(w_buf[last % 2, here, :], cg)

    for j in range(2):
        dkv_send[j] = kv_total(1 - core, j).astype(BF)
        dkv_copy(j).start()
    reduce(last - 1)
    kv_self = pltpu.make_async_copy(
        dkv_fin.at[pl.ds(pl.multiple_of(OUT_KEYS * t, OUT_KEYS), OUT_KEYS), :],
        kv_tiles.at[t], self_sem.at[1],
    )
    for j in range(2):
        whole = kv_total(core, j)
        dkv_copy(j).wait_recv()
        whole = whole + dkv_recv[j].astype(F32)
        rows = slice(j * HALF, (j + 1) * HALF)
        dkv_fin[rows, :] = jnp.where(row[rows] < length, whole, 0.0).astype(BF)

        def send(d, _):
            to = NT // 2 * j + (t + d) % (NT // 2)

            @pl.when(to != t)
            def _():
                kv_out(to, t).start()

            @pl.when(to == t)
            def _():
                kv_self.start()

            return 0

        lax.fori_loop(0, NT // 2, send, 0)
    reduce(last)

    kv_copy.wait_send()
    len_copy.wait_send()
    dkv_copy(0).wait_send()
    dkv_copy(1).wait_send()
    kv_self.wait()

    def drain_qg(pair, _):
        @pl.when(2 * pair + par != t)
        def _():
            qg_copy(pair).wait_send()

        return 0

    def drain_z(d, _):
        to = (z + d) % NZ
        for i in range(SLOTS):
            stat_copy(i, to, z).wait_send()
            dq_copy(i, to, z).wait_send()
        return 0

    def drain_dq(i, _):
        for half in range(2):
            for c in range(2):
                @pl.when(jnp.logical_not(own_piece(i, half, c)))
                def _():
                    dq_give(i, half, c).wait_send()

        return 0

    def drain_kv(d, _):
        kv_out((t + d) % NT, t).wait_send()
        return 0

    def arrive_kv(d, _):
        frm = (t + d) % NT
        kv_out(frm, frm).wait_recv()
        return 0

    def arrive_dq(frm, _):
        @pl.when(jnp.logical_or(frm != t, core == 1))
        def _():
            pltpu.make_async_remote_copy(
                src_ref=dq_fin.at[0, 0], dst_ref=dq_tiles.at[frm],
                send_sem=dqf_ssem.at[0, 0, 0], recv_sem=dqf_rsem.at[frm],
                device_id=(other, t), device_id_type=MESH,
            ).wait_recv()

        return 0

    lax.fori_loop(0, NT // 2, drain_qg, 0)
    lax.fori_loop(1, NZ, drain_z, 0)
    lax.fori_loop(0, SLOTS, drain_dq, 0)
    lax.fori_loop(1, NT, drain_kv, 0)
    lax.fori_loop(1, NT, arrive_kv, 0)
    lax.fori_loop(0, NT, arrive_dq, 0)


def assemble(kv_tiles, dq_tiles, dq_out, dk_out, dv_out):
    t = lax.axis_index("tok")
    left = lax.broadcasted_iota(jnp.int32, (1, PAIR), 1) < HEAD
    first = (t // 2) % 2 == 0
    for p in range(NT // 2):
        cols = slice(p * PAIR, (p + 1) * PAIR)
        a = kv_tiles[2 * p].astype(F32)
        b = kv_tiles[2 * p + 1].astype(F32)
        dk_out[:, cols] = jnp.where(left, a, pltpu.roll(b, HEAD, 1)).astype(BF)
        dv_out[:, cols] = jnp.where(left, pltpu.roll(a, HEAD, 1), b).astype(BF)
        a = dq_tiles[2 * p].astype(F32)[0:SMALL]
        b = dq_tiles[2 * p + 1].astype(F32)[0:SMALL]
        a = jnp.where(first, a, pltpu.roll(a, HEAD, 1))
        b = jnp.where(first, pltpu.roll(b, HEAD, 1), b)
        dq_out[:, cols] = jnp.where(left, a, b).astype(BF)


def local(queries, keys, values, grad_out, lengths):
    dma = pltpu.SemaphoreType.DMA
    vm = pltpu.VMEM
    kv_tiles, dq_tiles = pl.pallas_call(
        kernel,
        out_shape=(
            jax.ShapeDtypeStruct((NT, OUT_KEYS, PAIR), BF),
            jax.ShapeDtypeStruct((NT, PAD, PAIR), BF),
        ),
        in_specs=[pl.BlockSpec(memory_space=pltpu.SMEM)]
        + [pl.BlockSpec(memory_space=pl.ANY)] * 4,
        out_specs=(pl.BlockSpec(memory_space=pl.ANY),) * 2,
        scratch_shapes=[
            vm((ROWS, NT * HEAD), BF), vm((ROWS, NT * HEAD), BF),
            vm((KEYS, PAIR), BF), vm((KEYS, PAIR), BF),
            vm((2, PAIR, ROWS), BF), vm((NT // 2, PAIR, ROWS), BF),
            vm((SLOTS, 2, PAIR, ROWS), BF),
            vm((2, KEYS, PAIR), BF), vm((2, 8, PAIR), F32),
            vm((BOTH, PAIR), BF), vm((BOTH, PAIR), BF),
            vm((HEAD, BOTH), BF), vm((PAIR, BOTH), BF),
            vm((BOTH, BLOCK), F32), vm((2, BOTH, BLOCK), BF), vm((BOTH, BLOCK), BF),
            vm((BOTH, PAIR), F32), vm((SLOTS, NZ, 2, BLOCK), F32), vm((2, 1, BLOCK), F32),
            vm((SLOTS, ROWS, PAIR), BF), vm((SLOTS, NZ, PIECE, PAIR), BF),
            vm((SLOTS, 2, PAD, PAIR), BF),
            vm((2, HALF, PAIR), BF), vm((2, HALF, PAIR), BF), vm((KEYS, PAIR), BF),
            dma((4,)), dma((NT // 2,)), dma((NT // 2,)), dma((2,)), dma((2,)),
            dma((SLOTS, NZ)), dma((SLOTS, NZ)), dma((SLOTS, NZ)), dma((SLOTS, NZ)),
            dma((2,)), dma((2,)), dma((NT,)), dma((NT,)),
            dma((SLOTS, 2, 2)), dma((NT,)), dma((2,)),
        ],
        compiler_params=pltpu.CompilerParams(
            collective_id=0, has_side_effects=True, vmem_limit_bytes=56 * 2**20
        ),
    )(lengths, queries, grad_out, keys, values)
    return pl.pallas_call(
        assemble,
        out_shape=(
            jax.ShapeDtypeStruct((SMALL, NT * HEAD), BF),
            jax.ShapeDtypeStruct((OUT_KEYS, NT * HEAD), BF),
            jax.ShapeDtypeStruct((OUT_KEYS, NT * HEAD), BF),
        ),
        in_specs=[pl.BlockSpec(memory_space=pltpu.VMEM)] * 2,
        out_specs=(pl.BlockSpec(memory_space=pltpu.VMEM),) * 3,
    )(kv_tiles, dq_tiles)


def solution(mesh):
    in_specs = (P("tok", None), P("view", None), P("view", None), P("tok", None), P("view"))
    out_specs = (P(("tok", "view"), None), P(("view", "tok"), None), P(("view", "tok"), None))
    return jax.shard_map(local, mesh=mesh, in_specs=in_specs, out_specs=out_specs, check_vma=False)
```

time: 69.7 us -> 60.7 us (0.87)
  local copies, waits for them, and re-layouts: 4.56 us -> 0 us
  Pallas kernels: 63.6 us -> 59.3 us
    unnamed x3 -> x0, local copies, waits for them, and re-layouts: 4.56 us -> none
    pallas_call x1 -> x2, Pallas kernels: 63.6 us -> 59.3 us  [the longest x1 57.5 us: local(): pl.pallas_call(kernel, out_shape=(jax.ShapeDtypeStruct((NT, OUT_KEYS, PAI...]
where the time goes in v2:
time: 60.7 us; the launch traced here: 60.6 us
  Pallas kernels  59.3 us (98%)
  between operations  1.29 us (2%)
    pallas_call x1, Pallas kernels, local(): pl.pallas_call(kernel, out_shape=(jax.ShapeDtypeStruct((NT, OUT_KEYS, PAI...  57.5 us
    pallas_call x1, Pallas kernels, local(): pl.pallas_call(assemble, out_shape=(jax.ShapeDtypeStruct((SMALL, NT * HEA...  1.86 us

profile of v2, /device:TPU:1, one launch (start us, length us, event | category | flops | bytes accessed | tf_op | source)
XLA Modules:
  0.0 60.6 jit_solution(289982632243160656)
XLA Ops:
  1.3 57.5 %shard_map.76 = (bf16[16,64,128]{2,1,0:T(8,128)(2,1)}, bf16[16,32,128]{2,1,0:T(8,128)(2,1)}) custom-call(s32[1]{0:T(128)S(6)} %copy.8.len_ref, bf16[384,1024]{1,0:T(8,128)(2,1)} %q_hbm.1, bf16[384,1024]{1,0:T(8,128)(2,1)} %g_hbm.1, bf16[1024,1024]{1,0:T(8,128)(2,1)} %k_hbm.1, bf16[1024,1024]{1,0:T(8,128)(2,1)} %v_hbm.1), custom_call_target="tpu_custom_call" | custom-call | tf_op jit(solution)/shard_map/pallas_call | solution.py:482
  58.7 1.9 %shard_map.77 = (bf16[24,1024]{1,0:T(8,128)(2,1)}, bf16[64,1024]{1,0:T(8,128)(2,1)}, bf16[64,1024]{1,0:T(8,128)(2,1)}) custom-call(bf16[16,64,128]{2,1,0:T(8,128)(2,1)} %get-tuple-element.5.kv_tiles, bf16[16,32,128]{2,1,0:T(8,128)(2,1)} %get-tuple-element.6.dq_tiles), custom_call_target="tpu_custom_call" | custom-call | tf_op jit(solution)/shard_map/pallas_call | solution.py:513

commit v3 on v2

--- a/solution.py
+++ b/solution.py
@@ -19,9 +19,11 @@
 PIECE = ROWS // NZ
 SMALL = PIECE // 2
 OUT_KEYS = KEYS // NT
-STEP1 = 256
-STEP2 = 512
+STEP1 = 512
+LOG2E = 1.4426950408889634
+STEP2 = 1024
 HALF = 512
+ROW = KEYS // 4
 PAD = 32
 MESH = pl.DeviceIdType.MESH
 BF = jnp.bfloat16
@@ -37,8 +39,8 @@
     len_ref, q_hbm, g_hbm, k_hbm, v_hbm,
     kv_tiles, dq_tiles,
     q_v, g_v, k_v, v_v, turned, qgt, qg_buf, kv_buf, len_buf,
-    k0, v0, kt, vt1, s_ref, w_buf, ds_buf, dkv, stats, tops,
-    dq_send, dq_recv, dq_fin, dkv_send, dkv_recv, dkv_fin,
+    k0, v0, kt, vt1, s_ref, w_buf, ds_buf, cq_buf, cg_buf, stats, tops,
+    dq_send, dq_recv, dq_fin, dkv, dkv_send, dkv_recv, dkv_fin,
     load_sem, qg_ssem, qg_rsem, kv_ssem, kv_rsem, st_ssem, st_rsem,
     dq_ssem, dq_rsem, x_ssem, x_rsem, kvf_ssem, kvf_rsem, dqf_ssem, dqf_rsem, self_sem,
 ):
@@ -53,10 +55,10 @@
 
     pair_cols = pl.ds(pl.multiple_of(PAIR * (t // 2), PAIR), PAIR)
     loads = [
-        pltpu.make_async_copy(k_hbm.at[:, pair_cols], k_v, load_sem.at[0]),
-        pltpu.make_async_copy(v_hbm.at[:, pair_cols], v_v, load_sem.at[1]),
-        pltpu.make_async_copy(q_hbm, q_v, load_sem.at[2]),
-        pltpu.make_async_copy(g_hbm, g_v, load_sem.at[3]),
+        pltpu.make_async_copy(q_hbm, q_v, load_sem.at[0]),
+        pltpu.make_async_copy(g_hbm, g_v, load_sem.at[1]),
+        pltpu.make_async_copy(k_hbm.at[:, pair_cols], k_v, load_sem.at[2]),
+        pltpu.make_async_copy(v_hbm.at[:, pair_cols], v_v, load_sem.at[3]),
     ]
     for load in loads:
         load.start()
@@ -88,12 +90,51 @@
     lax.fori_loop(0, NT // 2, greet_other, 0)
     lax.fori_loop(1, NZ, greet_z, 0)
 
-    length = len_ref[0]
-    lane = lax.broadcasted_iota(jnp.int32, (1, PAIR), 1)
-    left = lane < HEAD
-    row = lax.broadcasted_iota(jnp.int32, (KEYS, 1), 0)
     loads[0].wait()
     loads[1].wait()
+    chosen = pl.ds(pl.multiple_of(HEAD * par, HEAD), HEAD)
+
+    def pack(j, _):
+        pair = (2 * y + j) % (NT // 2)
+        cols = pl.ds(pl.multiple_of(PAIR * pair, PAIR), PAIR)
+        turned[0] = q_v[:, cols].T
+        turned[1] = g_v[:, cols].T
+        qgt[pair, 0:HEAD, :] = turned[0, chosen, :]
+        qgt[pair, HEAD:PAIR, :] = turned[1, chosen, :]
+        return 0
+
+
+    lax.fori_loop(0, 2, pack, 0)
+    pl.semaphore_wait(barrier, 1 + NT - 1 + NT // 2 - (1 - core) + NZ - 1)
+
+    def qg_copy(pair):
+        return pltpu.make_async_remote_copy(
+            src_ref=qgt.at[pair], dst_ref=qg_buf.at[y, (t // 2) % 2],
+            send_sem=qg_ssem.at[pair], recv_sem=qg_rsem.at[t // 2],
+            device_id=(v, 2 * pair + par), device_id_type=MESH,
+        )
+
+    def send_row(j):
+        for half in range(2):
+            pair = 2 * ((y + j) % 4) + half
+
+            @pl.when(2 * pair + par != t)
+            def _():
+                qg_copy(pair).start()
+
+            @pl.when(2 * pair + par == t)
+            def _():
+                qg_buf[y, half] = qgt[pair]
+
+    send_row(0)
+    lax.fori_loop(2, 4, pack, 0)
+    send_row(1)
+
+    length = len_ref[0]
+    left = lax.broadcasted_iota(jnp.int32, (1, PAIR), 1) < HEAD
+    row = lax.broadcasted_iota(jnp.int32, (KEYS, 1), 0)
+    loads[2].wait()
+    loads[3].wait()
     even = t % 2 == 0
     k_f = k_v[...].astype(F32)
     v_f = v_v[...].astype(F32)
@@ -103,40 +144,6 @@
     kv = jnp.where(row < length, kv, kv[0:1, :])
     kv_buf[core] = kv.astype(BF)
     len_buf[core] = jnp.full((8, PAIR), length, jnp.int32).astype(F32)
-
-    loads[2].wait()
-    loads[3].wait()
-    chosen = pl.ds(pl.multiple_of(HEAD * par, HEAD), HEAD)
-
-    def pack(pair, _):
-        cols = pl.ds(pl.multiple_of(PAIR * pair, PAIR), PAIR)
-        turned[0] = q_v[:, cols].T
-        turned[1] = g_v[:, cols].T
-        qgt[pair, 0:HEAD, :] = turned[0, chosen, :]
-        qgt[pair, HEAD:PAIR, :] = turned[1, chosen, :]
-        return 0
-
-    lax.fori_loop(0, NT // 2, pack, 0)
-
-    col = lax.broadcasted_iota(jnp.int32, (1, KEYS), 1).astype(F32)
-    sub = lax.broadcasted_iota(jnp.int32, (HEAD, 1), 0)
-
-    def prepare(side):
-        here = pl.ds(pl.multiple_of(KEYS * side, KEYS), KEYS)
-        tile = kv_buf[side]
-        f = tile.astype(F32)
-        k0[here, :] = jnp.where(left, f, 0.0).astype(BF)
-        v0[here, :] = jnp.where(left, 0.0, f).astype(BF)
-        flipped = tile.T.astype(F32)
-        okay = jnp.where(col < len_buf[side][0:1, 0:1], 1.0, 0.0)
-        kt[:, here] = (flipped[0:HEAD] * okay).astype(BF)
-        vt1[HEAD:PAIR, here] = (flipped[HEAD:PAIR] * okay).astype(BF)
-        vt1[0:HEAD, here] = jnp.where(sub == 0, okay, 0.0).astype(BF)
-
-    prepare(core)
-    dkv[...] = jnp.zeros_like(dkv)
-
-    pl.semaphore_wait(barrier, 1 + NT - 1 + NT // 2 - (1 - core) + NZ - 1)
 
     kv_copy = pltpu.make_async_remote_copy(
         src_ref=kv_buf.at[core], dst_ref=kv_buf.at[core],
@@ -151,28 +158,25 @@
     kv_copy.start()
     len_copy.start()
 
-    def qg_copy(pair):
-        return pltpu.make_async_remote_copy(
-            src_ref=qgt.at[pair], dst_ref=qg_buf.at[y, (t // 2) % 2],
-            send_sem=qg_ssem.at[pair], recv_sem=qg_rsem.at[t // 2],
-            device_id=(v, 2 * pair + par), device_id_type=MESH,
-        )
-
-    def send_row(j):
-        for half in range(2):
-            pair = 2 * ((y + j) % 4) + half
-
-            @pl.when(2 * pair + par != t)
-            def _():
-                qg_copy(pair).start()
-
-            @pl.when(2 * pair + par == t)
-            def _():
-                qg_buf[y, half] = qgt[pair]
-
-    send_row(0)
-    send_row(1)
-
+    lax.fori_loop(4, NT // 2, pack, 0)
+
+    col = lax.broadcasted_iota(jnp.int32, (1, KEYS), 1).astype(F32)
+    sub = lax.broadcasted_iota(jnp.int32, (HEAD, 1), 0)
+
+    def prepare(side):
+        here = pl.ds(pl.multiple_of(KEYS * side, KEYS), KEYS)
+        tile = kv_buf[side]
+        f = tile.astype(F32)
+        k0[here, :] = jnp.where(left, f, 0.0).astype(BF)
+        v0[here, :] = jnp.where(left, 0.0, f).astype(BF)
+        flipped = tile.T.astype(F32)
+        okay = jnp.where(col < len_buf[side][0:1, 0:1], 1.0, 0.0)
+        kt[:, here] = (flipped[0:HEAD] * okay).astype(BF)
+        vt1[HEAD:PAIR, here] = (flipped[HEAD:PAIR] * okay).astype(BF)
+        vt1[0:HEAD, here] = jnp.where(sub == 0, okay, 0.0).astype(BF)
+
+
+    prepare(core)
     kv_copy.wait_recv()
     len_copy.wait_recv()
     prepare(1 - core)
@@ -192,6 +196,9 @@
             device_id=(2 * to + core, t), device_id_type=MESH,
         )
 
+    def far(d):
+        return NZ // 2 + (d // 2) * (2 * ((d + 1) % 2) - 1)
+
     def block_of(i):
         return (y + 3 * i) % 4
 
@@ -201,7 +208,6 @@
 
     def scores_phase(i):
         sb = block_of(i)
-        slot = i % 2
         for half in range(2):
             source = 4 * sb + 2 * half + par
 
@@ -225,21 +231,19 @@
             s_ref[here, :] = s
             top = jnp.maximum(top, jnp.max(s.reshape(STEP1 // 8, 8, BLOCK), axis=0))
         top = jnp.max(top, axis=0, keepdims=True)
-        acc = jnp.zeros((PAIR, BLOCK), F32)
         for k in range(BOTH // STEP1):
             here = slice(k * STEP1, (k + 1) * STEP1)
-            w = jnp.exp((s_ref[here, :] - top) * scale).astype(BF)
-            w_buf[slot, here, :] = w
-            acc = acc + mm(vt1[:, here], w)
+            w_buf[i, here, :] = jnp.exp2((s_ref[here, :] - top) * (scale * LOG2E)).astype(BF)
+        acc = mm(vt1[...], w_buf[i])
         total = acc[0:1, :]
         mean = jnp.sum(acc[HEAD:, :] * qg[HEAD:, :].astype(F32), axis=0, keepdims=True)
         top = top * scale
-        tops[slot] = top
+        tops[i] = top
         stats[i, z, 0:1, :] = top + jnp.log(total)
         stats[i, z, 1:2, :] = mean / total
 
         def send(d, _):
-            stat_copy(i, (z + d) % NZ, z).start()
+            stat_copy(i, (z + far(d)) % NZ, z).start()
             return 0
 
         lax.fori_loop(1, NZ, send, 0)
@@ -256,12 +260,12 @@
         weight = jnp.exp(logs - peak)
         total = jnp.sum(weight, axis=0, keepdims=True)
         mean = jnp.sum(stats[i, :, 1, :] * weight, axis=0, keepdims=True) / total
-        factor = jnp.exp(tops[i % 2] - peak) / total
+        factor = jnp.exp(tops[i] - peak) / total
         qg = queries_of(i)
         scaled = (qg.astype(F32) * factor).T
-        cq = jnp.where(left, scaled * scale, 0.0).astype(BF)
-        cg = jnp.where(left, 0.0, scaled).astype(BF)
-        return qg, mean, factor, cq, cg
+        cq_buf[i] = jnp.where(left, scaled * scale, 0.0).astype(BF)
+        cg_buf[i] = jnp.where(left, 0.0, scaled).astype(BF)
+        return qg, mean, factor
 
     def give_dq(i, acc, factor):
         acc = acc * (factor * scale)
@@ -269,22 +273,20 @@
         dq_send[i] = two.T.astype(BF)
 
         def send(d, _):
-            dq_copy(i, (z + d) % NZ, z).start()
+            dq_copy(i, (z + far(d)) % NZ, z).start()
             return 0
 
         lax.fori_loop(1, NZ, send, 0)
 
     def grads_phase(i):
-        slot = i % 2
-        qg, mean, factor, cq, cg = combine(i)
+        qg, mean, factor = combine(i)
         acc = jnp.zeros((HEAD, BLOCK), F32)
         for k in range(BOTH // STEP2):
             here = slice(k * STEP2, (k + 1) * STEP2)
             dp = mm(v0[here, :], qg)
-            w = w_buf[slot, here, :]
-            ds = (w.astype(F32) * (dp - mean)).astype(BF)
+            ds = (w_buf[i, here, :].astype(F32) * (dp - mean)).astype(BF)
+            ds_buf[i, here, :] = ds
             acc = acc + mm(kt[:, here], ds)
-            dkv[here, :] += mm(ds, cq) + mm(w, cg)
         give_dq(i, acc, factor)
 
     def dq_give(i, half, c):
@@ -326,35 +328,40 @@
                     keep.start()
                     keep.wait()
 
+    def kv_sum(here, blocks):
+        acc = jnp.zeros((here.size, PAIR), F32)
+        for i in blocks:
+            acc = acc + mm(ds_buf[i, here, :], cq_buf[i]) + mm(w_buf[i, here, :], cg_buf[i])
+        return acc
+
+    def mate_rows(j):
+        return pl.ds(pl.multiple_of(KEYS * (1 - core) + HALF * j, HALF), HALF)
+
     def turn(i, _):
-        scores_phase(i)
-
-        @pl.when(i > 0)
-        def _():
-            grads_phase(i - 1)
+        @pl.when(i < SLOTS)
+        def _():
+            scores_phase(i)
+
+        @pl.when(i == SLOTS + 1)
+        def _():
+            for j in range(2):
+                dkv[j] = kv_sum(mate_rows(j), (0, 1))
 
         @pl.when(i > 1)
         def _():
-            reduce(i - 2)
-
-        return 0
-
-    lax.fori_loop(0, SLOTS, turn, 0)
-
-    last = SLOTS - 1
-    qg, mean, factor, cq, cg = combine(last)
-    acc = jnp.zeros((HEAD, BLOCK), F32)
-    for k in range(BOTH // STEP2):
-        here = slice(k * STEP2, (k + 1) * STEP2)
-        dp = mm(v0[here, :], qg)
-        ds = (w_buf[last % 2, here, :].astype(F32) * (dp - mean)).astype(BF)
-        ds_buf[here, :] = ds
-        acc = acc + mm(kt[:, here], ds)
-    give_dq(last, acc, factor)
+            grads_phase(i - 2)
+
+        @pl.when(i > 3)
+        def _():
+            reduce(i - 4)
+
+        return 0
+
+    lax.fori_loop(0, SLOTS + 2, turn, 0)
 
     def dkv_copy(j):
         return pltpu.make_async_remote_copy(
-            src_ref=dkv_send.at[j], dst_ref=dkv_recv.at[j],
+            src_ref=dkv_send.at[j], dst_ref=dkv_recv.at[pl.ds(HALF * j, HALF), :],
             send_sem=x_ssem.at[j], recv_sem=x_rsem.at[j],
             device_id=(other, t), device_id_type=MESH,
         )
@@ -367,27 +374,32 @@
             device_id=(v, to), device_id_type=MESH,
         )
 
-    def kv_total(side, j):
-        here = pl.ds(pl.multiple_of(KEYS * side + HALF * j, HALF), HALF)
-        return dkv[here, :] + mm(ds_buf[here, :], cq) + mm(w_buf[last % 2, here, :], cg)
-
     for j in range(2):
-        dkv_send[j] = kv_total(1 - core, j).astype(BF)
+        dkv_send[j] = (dkv[j] + kv_sum(mate_rows(j), (2, 3))).astype(BF)
         dkv_copy(j).start()
-    reduce(last - 1)
+    reduce(SLOTS - 2)
     kv_self = pltpu.make_async_copy(
         dkv_fin.at[pl.ds(pl.multiple_of(OUT_KEYS * t, OUT_KEYS), OUT_KEYS), :],
         kv_tiles.at[t], self_sem.at[1],
     )
-    for j in range(2):
-        whole = kv_total(core, j)
-        dkv_copy(j).wait_recv()
-        whole = whole + dkv_recv[j].astype(F32)
-        rows = slice(j * HALF, (j + 1) * HALF)
-        dkv_fin[rows, :] = jnp.where(row[rows] < length, whole, 0.0).astype(BF)
+    row_of = lax.broadcasted_iota(jnp.int32, (ROW, 1), 0)
+
+    def own_rows(j, _):
+        to_y = (y + 2 + j * (1 + j) // 2) % 4
+        start = pl.multiple_of(ROW * to_y, ROW)
+        whole = kv_sum(pl.ds(pl.multiple_of(KEYS * core + start, ROW), ROW), range(SLOTS))
+
+        @pl.when(j == 0)
+        def _():
+            dkv_copy(0).wait_recv()
+            dkv_copy(1).wait_recv()
+
+        rows = pl.ds(start, ROW)
+        whole = whole + dkv_recv[rows, :].astype(F32)
+        dkv_fin[rows, :] = jnp.where(row_of + start < length, whole, 0.0).astype(BF)
 
         def send(d, _):
-            to = NT // 2 * j + (t + d) % (NT // 2)
+            to = 4 * to_y + (t + 2 + d) % 4
 
             @pl.when(to != t)
             def _():
@@ -399,8 +411,11 @@
 
             return 0
 
-        lax.fori_loop(0, NT // 2, send, 0)
-    reduce(last)
+        lax.fori_loop(0, 4, send, 0)
+        return 0
+
+    lax.fori_loop(0, 4, own_rows, 0)
+    reduce(SLOTS - 1)
 
     kv_copy.wait_send()
     len_copy.wait_send()
@@ -496,11 +511,13 @@
             vm((2, KEYS, PAIR), BF), vm((2, 8, PAIR), F32),
             vm((BOTH, PAIR), BF), vm((BOTH, PAIR), BF),
             vm((HEAD, BOTH), BF), vm((PAIR, BOTH), BF),
-            vm((BOTH, BLOCK), F32), vm((2, BOTH, BLOCK), BF), vm((BOTH, BLOCK), BF),
-            vm((BOTH, PAIR), F32), vm((SLOTS, NZ, 2, BLOCK), F32), vm((2, 1, BLOCK), F32),
+            vm((BOTH, BLOCK), F32), vm((SLOTS, BOTH, BLOCK), BF), vm((SLOTS, BOTH, BLOCK), BF),
+            vm((SLOTS, BLOCK, PAIR), BF), vm((SLOTS, BLOCK, PAIR), BF),
+            vm((SLOTS, NZ, 2, BLOCK), F32), vm((SLOTS, 1, BLOCK), F32),
             vm((SLOTS, ROWS, PAIR), BF), vm((SLOTS, NZ, PIECE, PAIR), BF),
             vm((SLOTS, 2, PAD, PAIR), BF),
-            vm((2, HALF, PAIR), BF), vm((2, HALF, PAIR), BF), vm((KEYS, PAIR), BF),
+            vm((2, HALF, PAIR), F32), vm((2, HALF, PAIR), BF),
+            vm((KEYS, PAIR), BF), vm((KEYS, PAIR), BF),
             dma((4,)), dma((NT // 2,)), dma((NT // 2,)), dma((2,)), dma((2,)),
             dma((SLOTS, NZ)), dma((SLOTS, NZ)), dma((SLOTS, NZ)), dma((SLOTS, NZ)),
             dma((2,)), dma((2,)), dma((NT,)), dma((NT,)),

time: 60.7 us -> 57 us (0.939)
  Pallas kernels: 59.3 us -> 55.6 us
    pallas_call x1, Pallas kernels: 57.5 us -> 53.7 us  [local(): pl.pallas_call(kernel, out_shape=(jax.ShapeDtypeStruct((NT, OUT_KEYS, PAI...]
where the time goes in v3:
time: 57 us; the launch traced here: 56.8 us
  Pallas kernels  55.6 us (98%)
  between operations  1.29 us (2%)
    pallas_call x1, Pallas kernels, local(): pl.pallas_call(kernel, out_shape=(jax.ShapeDtypeStruct((NT, OUT_KEYS, PAI...  53.7 us
    pallas_call x1, Pallas kernels, local(): pl.pallas_call(assemble, out_shape=(jax.ShapeDtypeStruct((SMALL, NT * HEA...  1.86 us

profile of v3, /device:TPU:1, one launch (start us, length us, event | category | flops | bytes accessed | tf_op | source)
XLA Modules:
  0.0 56.8 jit_solution(13534975208896747532)
XLA Ops:
  1.3 53.7 %shard_map.76 = (bf16[16,64,128]{2,1,0:T(8,128)(2,1)}, bf16[16,32,128]{2,1,0:T(8,128)(2,1)}) custom-call(s32[1]{0:T(128)S(6)} %copy.8.len_ref, bf16[384,1024]{1,0:T(8,128)(2,1)} %q_hbm.1, bf16[384,1024]{1,0:T(8,128)(2,1)} %g_hbm.1, bf16[1024,1024]{1,0:T(8,128)(2,1)} %k_hbm.1, bf16[1024,1024]{1,0:T(8,128)(2,1)} %v_hbm.1), custom_call_target="tpu_custom_call" | custom-call | tf_op jit(solution)/shard_map/pallas_call | solution.py:497
  55.0 1.9 %shard_map.77 = (bf16[24,1024]{1,0:T(8,128)(2,1)}, bf16[64,1024]{1,0:T(8,128)(2,1)}, bf16[64,1024]{1,0:T(8,128)(2,1)}) custom-call(bf16[16,64,128]{2,1,0:T(8,128)(2,1)} %get-tuple-element.5.kv_tiles, bf16[16,32,128]{2,1,0:T(8,128)(2,1)} %get-tuple-element.6.dq_tiles), custom_call_target="tpu_custom_call" | custom-call | tf_op jit(solution)/shard_map/pallas_call | solution.py:530

commit v4 on v3

--- a/solution.py
+++ b/solution.py
@@ -94,8 +94,12 @@
     loads[1].wait()
     chosen = pl.ds(pl.multiple_of(HEAD * par, HEAD), HEAD)
 
+    def row_at(i):
+        i = jnp.int32(i)
+        return i + jnp.where(i == 1, 1, 0) - jnp.where(i == 2, 1, 0)
+
     def pack(j, _):
-        pair = (2 * y + j) % (NT // 2)
+        pair = 2 * ((y + row_at(j // 2)) % 4) + j % 2
         cols = pl.ds(pl.multiple_of(PAIR * pair, PAIR), PAIR)
         turned[0] = q_v[:, cols].T
         turned[1] = g_v[:, cols].T
@@ -116,7 +120,7 @@
 
     def send_row(j):
         for half in range(2):
-            pair = 2 * ((y + j) % 4) + half
+            pair = 2 * ((y + row_at(j)) % 4) + half
 
             @pl.when(2 * pair + par != t)
             def _():
@@ -200,7 +204,7 @@
         return NZ // 2 + (d // 2) * (2 * ((d + 1) % 2) - 1)
 
     def block_of(i):
-        return (y + 3 * i) % 4
+        return (y + 4 - row_at(i)) % 4
 
     def queries_of(i):
         sb = block_of(i)
@@ -384,37 +388,21 @@
     )
     row_of = lax.broadcasted_iota(jnp.int32, (ROW, 1), 0)
 
-    def own_rows(j, _):
-        to_y = (y + 2 + j * (1 + j) // 2) % 4
+    for j in range(4):
+        to_y = (y + (2, 3, 1, 0)[j]) % 4
         start = pl.multiple_of(ROW * to_y, ROW)
         whole = kv_sum(pl.ds(pl.multiple_of(KEYS * core + start, ROW), ROW), range(SLOTS))
-
-        @pl.when(j == 0)
-        def _():
+        if j == 0:
             dkv_copy(0).wait_recv()
             dkv_copy(1).wait_recv()
-
         rows = pl.ds(start, ROW)
         whole = whole + dkv_recv[rows, :].astype(F32)
         dkv_fin[rows, :] = jnp.where(row_of + start < length, whole, 0.0).astype(BF)
-
-        def send(d, _):
-            to = 4 * to_y + (t + 2 + d) % 4
-
-            @pl.when(to != t)
-            def _():
-                kv_out(to, t).start()
-
-            @pl.when(to == t)
-            def _():
+        for d in (2, 1, 3, 0):
+            if j == 3 and d == 0:
                 kv_self.start()
-
-            return 0
-
-        lax.fori_loop(0, 4, send, 0)
-        return 0
-
-    lax.fori_loop(0, 4, own_rows, 0)
+            else:
+                kv_out(4 * to_y + (t + d) % 4, t).start()
     reduce(SLOTS - 1)
 
     kv_copy.wait_send()

time: 57 us -> 55.5 us (0.974)
  Pallas kernels: 55.6 us -> 54.1 us
    pallas_call x1, Pallas kernels: 53.7 us -> 52.2 us  [local(): pl.pallas_call(kernel, out_shape=(jax.ShapeDtypeStruct((NT, OUT_KEYS, PAI...]
where the time goes in v4:
time: 55.5 us; the launch traced here: 55.4 us
  Pallas kernels  54.1 us (97%)
  between operations  1.29 us (2%)
    pallas_call x1, Pallas kernels, local(): pl.pallas_call(kernel, out_shape=(jax.ShapeDtypeStruct((NT, OUT_KEYS, PAI...  52.2 us
    pallas_call x1, Pallas kernels, local(): pl.pallas_call(assemble, out_shape=(jax.ShapeDtypeStruct((SMALL, NT * HEA...  1.86 us

profile of v4, /device:TPU:1, one launch (start us, length us, event | category | flops | bytes accessed | tf_op | source)
XLA Modules:
  0.0 55.4 jit_solution(5741684722597061904)
XLA Ops:
  1.3 52.2 %shard_map.76 = (bf16[16,64,128]{2,1,0:T(8,128)(2,1)}, bf16[16,32,128]{2,1,0:T(8,128)(2,1)}) custom-call(s32[1]{0:T(128)S(6)} %copy.8.len_ref, bf16[384,1024]{1,0:T(8,128)(2,1)} %q_hbm.1, bf16[384,1024]{1,0:T(8,128)(2,1)} %g_hbm.1, bf16[1024,1024]{1,0:T(8,128)(2,1)} %k_hbm.1, bf16[1024,1024]{1,0:T(8,128)(2,1)} %v_hbm.1), custom_call_target="tpu_custom_call" | custom-call | tf_op jit(solution)/shard_map/pallas_call | solution.py:485
  53.5 1.9 %shard_map.77 = (bf16[24,1024]{1,0:T(8,128)(2,1)}, bf16[64,1024]{1,0:T(8,128)(2,1)}, bf16[64,1024]{1,0:T(8,128)(2,1)}) custom-call(bf16[16,64,128]{2,1,0:T(8,128)(2,1)} %get-tuple-element.5.kv_tiles, bf16[16,32,128]{2,1,0:T(8,128)(2,1)} %get-tuple-element.6.dq_tiles), custom_call_target="tpu_custom_call" | custom-call | tf_op jit(solution)/shard_map/pallas_call | solution.py:518
